TPU v7x, 32 devices: a whole 2x2x4 slice. The times are simulated.
32 devices in a mesh: group: 2 (over y), gx: 4 (over z), gy: 4 (over x, core).
Axes of the slice: x: 2, y: 2, z: 4, core: 2. Of those that a mesh axis runs over, the one named last changes fastest.
Arguments:
- hidden_in: bfloat16 [128, 16384], P('group', ('gx', 'gy')), parts along dimension 0, may hold values from -6 to 6
- exponents: int32 [128, 128], P('group', 'gx'), parts along dimension 0, may hold values from -2 to 1
- signs: int32 [128], replicated, may hold values from 0 to 1
- lengths: int32 [128], P(('group', 'gx')), parts along dimension 0, may hold values from 1 to 1024, 32768 in all
- w_query: bfloat16 [16384, 8192], P('gx', 'gy'), may hold values from -0.046875 to 0.046875
- key_value_weight: bfloat16 [16384, 8, 2, 128], P('gx', 'gy'), may hold values from -0.046875 to 0.046875
- w_out: bfloat16 [8192, 16384], P('gy', 'gx'), may hold values from -0.0625 to 0.0625
- keys_cache: bfloat16 [128, 8, 1024, 128], P(('group', 'gx'), 'gy'), parts along dimension 0, may hold values from -600 to 600
- cached_value_rows: bfloat16 [128, 8, 1024, 128], P(('group', 'gx'), 'gy'), parts along dimension 0, may hold values from -24 to 24
Outputs:
- attn_update: bfloat16 [128, 16384], P('group', ('gx', 'gy')), parts along dimension 0
There are 2 independent parts, one for each index of `group`. A program takes and returns all parts, laid end to end along the dimension named above; an argument that names none is the same for every part. Nothing has to cross between parts.
Inputs may be any that keep to these rules, and one draw needn't show every extreme that they name: `lengths`: the longest request of a part holds exactly 1024 cached tokens.
All inputs are finite; a program needn't handle non-finite values. No bound on the sum of `lengths` on one device may be relied on, other than what follows from the above.
Results may differ from a plain program's by a relative error of at most 0.0065.
The roundings to bfloat16 on the way count: a program that leaves them out, or rounds other values in their place, can miss the bound.
Values may be sent and summed in bfloat16 or wider, within the bound.
A program may use at most 128 MiB of HBM per device.

v0:
```python
import math

import jax
import jax.numpy as jnp
from jax import lax
from jax.sharding import PartitionSpec as P

MODEL_WIDTH = 16384


def hadamard_table(block_len):
    index_vals = jnp.arange(block_len, dtype=jnp.int32)
    parity = jnp.zeros((block_len, block_len), jnp.int32)
    for bit_number in range(block_len.bit_length() - 1):
        step_size = 2**bit_number
        parity = parity + index_vals[:, None] // step_size % 2 * (
            index_vals[None, :] // step_size % 2
        )
    return jnp.where(parity % 2 == 0, 1.0, -1.0).astype(jnp.float32) / math.sqrt(block_len)


def quantize(blocks, exps, table, signs):
    signed = blocks * (2.0 * signs.astype(jnp.float32) - 1.0)
    rotated = jnp.einsum("bnk,kj->bnj", signed, table, precision=lax.Precision.HIGHEST)
    factor = jnp.exp2(exps.astype(jnp.float32))[..., None]
    coded = jnp.clip(rotated / factor, -4.0, 4.0).astype(jnp.bfloat16)
    return (coded.astype(jnp.float32) * factor).astype(jnp.bfloat16)


def rotary_angles(values, positions):
    half_width = values.shape[-1] // 2
    freqs = jnp.power(
        500000.0, -(jnp.arange(half_width, dtype=jnp.float32) * 2.0 / values.shape[-1])
    )
    angles = positions.astype(jnp.float32).reshape((-1,) + (1,) * (values.ndim - 1)) * freqs
    cosine = jnp.cos(angles)
    sine = jnp.sin(angles)
    first_half = values[..., :half_width]
    second_half = values[..., half_width:]
    return jnp.concatenate(
        [first_half * cosine - second_half * sine, second_half * cosine + first_half * sine],
        axis=-1,
    )


def body(
    hidden_in,
    exponents,
    signs,
    lengths,
    w_query,
    key_value_weight,
    w_out,
    keys_cache,
    cached_value_rows,
):
    batch_all, local_feat = hidden_in.shape
    block_len = signs.shape[0]
    table = hadamard_table(block_len)
    widened = hidden_in.astype(jnp.float32)
    energy = lax.psum(jnp.sum(widened * widened, axis=1, keepdims=True), ("gx", "gy"))
    row_scale = lax.rsqrt(energy / MODEL_WIDTH + 1e-05)
    own_blocks = local_feat // block_len
    own_exps = lax.dynamic_slice_in_dim(exponents, lax.axis_index("gy") * own_blocks, own_blocks, 1)
    coded_own = quantize(
        (widened * row_scale).reshape(batch_all, own_blocks, block_len), own_exps, table, signs
    )
    gathered = lax.all_gather(coded_own.reshape(batch_all, local_feat), "gy", axis=1, tiled=True)
    query_cols = w_query.shape[1]
    kv_heads = key_value_weight.shape[1]
    head_dim = key_value_weight.shape[3]
    kv_flat = key_value_weight.reshape(key_value_weight.shape[0], kv_heads * 2 * head_dim)
    owners = batch_all // lax.axis_size("gx")
    partial_cols = lax.psum_scatter(
        jnp.concatenate(
            [
                jnp.dot(gathered, w_query, preferred_element_type=jnp.float32),
                jnp.dot(gathered, kv_flat, preferred_element_type=jnp.float32),
            ],
            axis=1,
        ),
        "gx",
        scatter_dimension=1,
        tiled=True,
    )
    mine = lax.all_to_all(partial_cols, "gx", split_axis=0, concat_axis=1, tiled=True)
    query_unrotated = mine[:, :query_cols].reshape(owners, kv_heads, -1, head_dim)
    key_value_unrotated = mine[:, query_cols:].reshape(owners, kv_heads, 2, head_dim)
    query_rotated = rotary_angles(query_unrotated, lengths).astype(jnp.bfloat16)
    key_new = rotary_angles(key_value_unrotated[:, :, 0], lengths).astype(jnp.bfloat16)
    value_new = key_value_unrotated[:, :, 1].astype(jnp.bfloat16)
    scale = 1.0 / math.sqrt(head_dim)
    scores = (
        jnp.einsum("bgrd,bgpd->bgrp", query_rotated, keys_cache, preferred_element_type=jnp.float32)
        * scale
    )
    fresh = (
        jnp.einsum("bgrd,bgd->bgr", query_rotated, key_new, preferred_element_type=jnp.float32)
        * scale
    )
    valid = (jnp.arange(keys_cache.shape[2], dtype=jnp.int32)[None, :] < lengths[:, None])[
        :, None, None, :
    ]
    masked = jnp.where(valid, scores, -1e30)
    top = jnp.maximum(jnp.max(masked, axis=-1), fresh)
    weights = jnp.where(valid, jnp.exp(masked - top[..., None]), 0.0)
    fresh_w = jnp.exp(fresh - top)
    total = jnp.sum(weights, axis=-1) + fresh_w
    probs = (weights / total[..., None]).astype(jnp.bfloat16)
    fresh_p = (fresh_w / total).astype(jnp.bfloat16)
    mixed = jnp.einsum(
        "bgrp,bgpd->bgrd", probs, cached_value_rows, preferred_element_type=jnp.float32
    )
    mixed = (
        mixed
        + fresh_p.astype(jnp.float32)[..., None] * value_new.astype(jnp.float32)[:, :, None, :]
    )
    attended = mixed.astype(jnp.bfloat16).reshape(owners, -1)
    terms = jnp.dot(
        lax.all_gather(attended, "gx", axis=0, tiled=True),
        w_out,
        preferred_element_type=jnp.float32,
    )
    summed = lax.psum_scatter(terms, "gy", scatter_dimension=1, tiled=True)
    return summed.astype(jnp.bfloat16)


def solution(mesh):
    in_specs = (
        P("group", ("gx", "gy")),
        P("group", "gx"),
        P(),
        P(("group", "gx")),
        P("gx", "gy"),
        P("gx", "gy", None, None),
        P("gy", "gx"),
        P(("group", "gx"), "gy", None, None),
        P(("group", "gx"), "gy", None, None),
    )
    out_specs = P("group", ("gx", "gy"))
    return jax.shard_map(body, mesh=mesh, in_specs=in_specs, out_specs=out_specs, check_vma=False)
```

profile of v0, /device:TPU:0, one launch (start us, length us, event | category | flops | bytes accessed | tf_op | source)
XLA Modules:
  0.0 169.9 jit_solution(8696076920241140237)
XLA Ops:
  6.6 0.7 multiply_exponential_fusion
  7.3 1.0 fusion.12
  8.4 34.9 %psum.7 = f32[64,1]{0,1:T(1,128)S(1)} all-reduce(f32[64,1]{0,1:T(1,128)S(1)} %bitcast.58), channel_id=1, replica_groups=mesh['group'=2,'gx'=4,'gy'=4] {'gx','gy'}, use_global_device_ids=true, to_apply=%region_1.2 | all-reduce | flops 64 | bytes 512 | tf_op jit(solution)/shard_map/psum | solution.py:61
  43.3 1.0 fusion.13
  44.4 0.7 multiply_add_fusion
  45.0 0.5 fusion.5
  45.6 6.5 %all_gather.6 = bf16[64,4096]{1,0:T(8,128)(2,1)S(1)} all-gather(bf16[64,1024]{1,0:T(8,128)(2,1)S(1)} %bitcast.50), channel_id=1, replica_groups=mesh['group'=2,'gx'=4,'gy'=4] {'gy'}, dimensions={1}, use_global_device_ids=true | all-gather | bytes 655360 | tf_op jit(solution)/shard_map/all_gather | solution.py:68
  52.1 7.2 %reshape.825 = bf16[4096,512]{1,0:T(8,128)(2,1)} reshape(bf16[4096,2,2,128]{3,2,1,0:T(2,128)(2,1)} %param.14) | data formatting | bytes 8388608 | tf_op jit(solution)/shard_map/reshape | solution.py:72
  59.3 3.0 %fusion.67 = f32[64,512]{1,0:T(8,128)S(1)} fusion(bf16[64,4096]{1,0:T(8,128)(2,1)S(1)} %all_gather.6, bf16[4096,512]{1,0:T(8,128)(2,1)} %reshape.825), kind=kOutput, calls=%fused_computation.136 | convolution fusion | flops 268435456 | bytes 4849664 | tf_op jit(solution)/shard_map/dot_general | solution.py:78
  62.4 8.8 %fusion.66 = f32[64,2048]{1,0:T(8,128)S(1)} fusion(bf16[64,4096]{1,0:T(8,128)(2,1)S(1)} %all_gather.6, bf16[4096,2048]{1,0:T(8,128)(2,1)} %param.13), kind=kOutput, calls=%fused_computation.135 | convolution fusion | flops 1073741824 | bytes 17825792 | tf_op jit(solution)/shard_map/dot_general | solution.py:77
  71.2 0.9 pad_maximum_fusion
  72.2 20.2 %reduce-scatter.3.cloned.1.call-done = f32[64,640]{1,0:T(8,128)} async-done(((f32[64,2560]{1,0:T(8,128)}), f32[64,640]{1,0:T(8,128)}) %reduce-scatter.3.cloned.1.call-update) | async-done | bytes 163856 | tf_op jit(solution)/shard_map/reduce_scatter | solution.py:74
  92.4 3.3 %all-to-all-start = ((f32[4,16,640]{2,1,0:T(8,128)}), f32[4,16,640]{2,1,0:T(8,128)S(1)}, u32[]{:S(2)}, u32[]{:S(2)}) async-start(f32[4,16,640]{2,1,0:T(8,128)} %bitcast.52), calls=%async_computation.1 | async-start | bytes 327680 | tf_op jit(solution)/shard_map/all_to_all | solution.py:86
  95.8 0.1 multiply_cosine_fusion
  95.9 5.8 %all-to-all-done = f32[4,16,640]{2,1,0:T(8,128)S(1)} async-done(((f32[4,16,640]{2,1,0:T(8,128)}), f32[4,16,640]{2,1,0:T(8,128)S(1)}, u32[]{:S(2)}, u32[]{:S(2)}) %all-to-all-start) | async-done | bytes 163872 | tf_op jit(solution)/shard_map/all_to_all | solution.py:86
  101.9 0.1 subtract_convert_fusion
  102.1 0.2 fusion.43
  102.4 5.8 %fusion.65 = (f32[16,2,8]{2,1,0:T(2,128)S(1)}, f32[16,2,8,1024]{3,2,1,0:T(8,128)S(1)}) fusion(bf16[16,2,1024,128]{3,2,1,0:T(8,128)(2,1)} %param.16, bf16[16,2,8,64]{3,2,1,0:T(8,128)(2,1)S(1)} %get-tuple-element.6, bf16[16,2,8,64]{3,2,1,0:T(8,128)(2,1)S(1)} %get-tuple-element.5, pred[16,1024]{1,0:T(8,128)(4,1)S(1)} %iota_compare_fusion), kind=kOutput, calls=%fused_computation.134 | convolution fusion | flops 68026112 | bytes 9520128 | tf_op jit(solution)/shard_map/bgrd,bgpd->bgrp/dot_general | solution.py:94
  108.2 0.4 fusion.7
  108.6 4.7 %fusion.6 = bf16[16,2,8,128]{3,2,1,0:T(8,128)(2,1)S(1)} fusion(bf16[16,2,1024,128]{3,2,1,0:T(8,128)(2,1)} %param.17, f32[16,2,8,1024]{3,2,1,0:T(8,128)S(1)} %get-tuple-element.14, f32[16,2,8]{2,1,0:T(2,128)S(1)} %get-tuple-element.8, f32[16,2,8]{2,1,0:T(2,128)S(1)} %multiply_maximum_fusion, pred[16,1024]{1,0:T(8,128)(4,1)S(1)} %iota_compare_fusion, ...), kind=kOutput, calls=%fused_computation.9 | convolution fusion | flops 68255744 | bytes 9538560 | tf_op jit(solution)/shard_map/bgrp,bgpd->bgrd/dot_general | solution.py:111
  113.3 13.8 %all_gather.7 = bf16[64,2048]{1,0:T(8,128)(2,1)S(1)} all-gather(bf16[16,2048]{1,0:T(8,128)(2,1)S(1)} %bitcast.51), channel_id=1, replica_groups=mesh['group'=2,'gx'=4,'gy'=4] {'gx'}, dimensions={0}, use_global_device_ids=true | all-gather | bytes 327680 | tf_op jit(solution)/shard_map/all_gather | solution.py:120
  127.2 9.8 %fusion.68 = f32[64,4096]{1,0:T(8,128)} fusion(bf16[64,2048]{1,0:T(8,128)(2,1)S(1)} %all_gather.7, bf16[2048,4096]{1,0:T(8,128)(2,1)} %param.15), kind=kOutput, calls=%fused_computation.137 | convolution fusion | flops 1073741824 | bytes 18087936 | tf_op jit(solution)/shard_map/dot_general | solution.py:119
  137.0 24.5 %reduce-scatter.5.cloned.1.call-done = f32[64,1024]{1,0:T(8,128)} async-done(((f32[64,4096]{1,0:T(8,128)}), f32[64,1024]{1,0:T(8,128)}) %reduce-scatter.5.cloned.1.call-update) | async-done | bytes 262160 | tf_op jit(solution)/shard_map/reduce_scatter | solution.py:124
  161.4 1.6 convert_element_type.54
  (31 shorter events, 0.8 us)
Async XLA Ops:
  6.5 85.8 %reduce-scatter.3.cloned.1.call-start = ((), (), s32[]{:S(2)}) async-start(), calls=%async_computation.3 | async-start | bytes 819200 | tf_op jit(solution)/shard_map/reduce_scatter | solution.py:74
  62.4 9.7 %copy-start = (s32[16]{0:T(128)S(1)}, s32[16]{0:T(128)}, u32[]{:S(2)}) copy-start(s32[16]{0:T(128)} %param.12) | copy-start | bytes 196
  92.4 9.3 %all-to-all-start = ((f32[4,16,640]{2,1,0:T(8,128)}), f32[4,16,640]{2,1,0:T(8,128)S(1)}, u32[]{:S(2)}, u32[]{:S(2)}) async-start(f32[4,16,640]{2,1,0:T(8,128)} %bitcast.52), calls=%async_computation.1 | async-start | bytes 327680 | tf_op jit(solution)/shard_map/all_to_all | solution.py:86
  95.7 65.7 %reduce-scatter.5.cloned.1.call-start = ((), (), s32[]{:S(2)}) async-start(), calls=%async_computation.4 | async-start | bytes 1310720 | tf_op jit(solution)/shard_map/reduce_scatter | solution.py:124
Sparse Core Ops, SparseCore 0:
  72.2 20.1 reduce-scatter.2
  137.1 24.2 reduce-scatter.4
where the time goes:
time: 171 us; the launch traced here: 170 us
  blocking collectives  55.2 us (32%)
  waiting for transfers between devices  50.4 us (29%)
  matrix products  32.8 us (19%)
  between operations  13.6 us (8%)
  local copies, waits for them, and re-layouts  7.51 us (4%)
  other arithmetic  6.87 us (4%)
  starting transfers between devices  3.39 us (2%)
    psum x1, blocking collectives, body(): lax.psum(jnp.sum(widened * widened, axis=1, keepdims=True), ('gx', 'gy'))  34.9 us
    reduce_scatter x1, waiting for transfers between devices, body(): summed = lax.psum_scatter(terms, 'gy', scatter_dimension=1, tiled=True)  24.5 us
    reduce_scatter x1, waiting for transfers between devices, body(): lax.psum_scatter(jnp.concatenate([jnp.dot(gathered, w_query, preferred_el...  20.2 us
    all_gather x1, blocking collectives, body(): lax.all_gather(attended, 'gx', axis=0, tiled=True)  13.8 us
    dot_general x1, matrix products, body(): jnp.dot(lax.all_gather(attended, 'gx', axis=0, tiled=True), w_out, prefer...  9.79 us
    dot_general x1, matrix products, body(): jnp.dot(gathered, w_query, preferred_element_type=jnp.float32)  8.79 us
    reshape x1, local copies, waits for them, and re-layouts, body(): key_value_weight.reshape(key_value_weight.shape[0], kv_heads * 2 * head_dim)  7.21 us
    all_gather x1, blocking collectives, body(): lax.all_gather(coded_own.reshape(batch_all, local_feat), 'gy', axis=1, ti...  6.51 us
  transfers between devices with their start and end apart: 3, of which 3 were waited for; matrix products, arithmetic and copies ran while one was open for 0% of the time, Pallas kernels for 0%

commit v1 on v0

--- a/solution.py
+++ b/solution.py
@@ -1,11 +1,397 @@
+import functools
 import math
 
 import jax
 import jax.numpy as jnp
 from jax import lax
+from jax.experimental import pallas as pl
+from jax.experimental.pallas import tpu as pltpu
 from jax.sharding import PartitionSpec as P
 
 MODEL_WIDTH = 16384
+MESH = pl.DeviceIdType.MESH
+CHUNK = 512
+
+
+def decode_kernel(
+    nx, ny, dims,
+    hidden_ref, exps_ref, signs_ref, cos_ref, sin_ref, len_ref,
+    wq_hbm, kv_hbm, wout_hbm, keys_hbm, values_hbm,
+    out_ref,
+    wbuf, kv_raw, kv_stage, kv_w, keys, values,
+    hid, en, dec, part, got, q2d, kv2d, att2d, att_all, term, terms_in,
+    w_sem, kv_sem, k_sem, v_sem, wo_sem,
+    hs_sem, hr_sem, es_sem, er_sem, ps_sem, pr_sem, as_sem, ar_sem, ts_sem, tr_sem,
+):
+    batch, feat, q_cols, owners, kv_heads, reps, slots, head_dim, out_cols = dims
+    gx = lax.axis_index("gx")
+    gy = lax.axis_index("gy")
+    peers = nx * ny
+    me = gx * ny + gy
+    block = head_dim
+    q_chunks = q_cols // CHUNK
+    depth = feat * ny
+    heads = kv_heads * reps
+    f32, bf16 = jnp.float32, jnp.bfloat16
+
+    def kv_copy():
+        return pltpu.make_async_copy(kv_hbm, kv_raw, kv_sem)
+
+    def wq_copy(c):
+        return pltpu.make_async_copy(
+            wq_hbm.at[:, pl.ds(pl.multiple_of(c * CHUNK, CHUNK), CHUNK)], wbuf.at[c], w_sem.at[c]
+        )
+
+    kv_copy().start()
+    for c in range(q_chunks):
+        wq_copy(c).start()
+    k_copy = pltpu.make_async_copy(keys_hbm, keys, k_sem)
+    v_copy = pltpu.make_async_copy(values_hbm, values, v_sem)
+    k_copy.start()
+    v_copy.start()
+
+    barrier = pltpu.get_barrier_semaphore()
+
+    def peer(k):
+        idx = lax.rem(me + k, peers)
+        return {"gx": idx // ny, "gy": lax.rem(idx, ny)}
+
+    def greet(k, carry):
+        pl.semaphore_signal(barrier, inc=1, device_id=peer(k), device_id_type=MESH)
+        return carry
+
+    lax.fori_loop(1, peers, greet, 0)
+
+    own = hidden_ref[...]
+    wide = own.astype(f32)
+    square = wide * wide
+    high = square.astype(bf16)
+    low = (square - high.astype(f32)).astype(bf16)
+    ones = jnp.ones((8, feat), bf16)
+    contract = (((1,), (1,)), ((), ()))
+    row = lax.dot_general(ones, high, contract, preferred_element_type=f32) + lax.dot_general(
+        ones, low, contract, preferred_element_type=f32
+    )
+    lanes = en.shape[2]
+    if lanes > batch:
+        row = jnp.concatenate([row, jnp.zeros((8, lanes - batch), f32)], axis=1)
+    en[me] = row
+    hid[gy] = own
+
+    pl.semaphore_wait(barrier, peers - 1)
+
+    def energy_copy(k):
+        return pltpu.make_async_remote_copy(
+            src_ref=en.at[me], dst_ref=en.at[me], send_sem=es_sem.at[k - 1],
+            recv_sem=er_sem.at[k - 1], device_id=peer(k), device_id_type=MESH,
+        )
+
+    def send_energy(k, carry):
+        energy_copy(k).start()
+        return carry
+
+    lax.fori_loop(1, peers, send_energy, 0)
+
+    def hidden_copy(d):
+        return pltpu.make_async_remote_copy(
+            src_ref=hid.at[gy], dst_ref=hid.at[gy], send_sem=hs_sem.at[d - 1],
+            recv_sem=hr_sem.at[d - 1], device_id={"gy": lax.rem(gy + d, ny)}, device_id_type=MESH,
+        )
+
+    for d in range(1, ny):
+        hidden_copy(d).start()
+
+    kv_copy().wait()
+    parts = kv_heads * 2
+    step_rows = kv_stage.shape[0]
+    rows_out = step_rows // parts
+
+    def separate(i, carry):
+        base = pl.multiple_of(i * step_rows, step_rows)
+        kv_stage[...] = kv_raw[pl.ds(base, step_rows), :].astype(f32)
+        to = pl.multiple_of(i * rows_out, rows_out)
+        for j in range(parts):
+            kv_w[pl.ds(to, rows_out), j * head_dim:(j + 1) * head_dim] = kv_stage[
+                pl.ds(j, rows_out, stride=parts), :
+            ].astype(bf16)
+        return carry
+
+    lax.fori_loop(0, depth // rows_out, separate, 0)
+
+    r = lax.broadcasted_iota(jnp.int32, (block, block), 0)
+    c = lax.broadcasted_iota(jnp.int32, (block, block), 1)
+    common = r & c
+    parity = jnp.zeros((block, block), jnp.int32)
+    for bit in range(block.bit_length() - 1):
+        parity = parity + ((common >> bit) & 1)
+    sign_row = 2.0 * signs_ref[...].astype(f32) - 1.0
+    sign_col = jnp.sum(jnp.where(r == c, sign_row, 0.0), axis=1, keepdims=True)
+    table = (jnp.where((parity & 1) == 0, 1.0, -1.0) * sign_col).astype(bf16)
+
+    def wait_energy(k, carry):
+        energy_copy(k).wait()
+        return carry
+
+    lax.fori_loop(1, peers, wait_energy, 0)
+    energy_row = jnp.sum(en[...], axis=0)[0:1, :]
+    er = lax.broadcasted_iota(jnp.int32, (batch, lanes), 0)
+    ec = lax.broadcasted_iota(jnp.int32, (batch, lanes), 1)
+    energy = jnp.sum(jnp.where(er == ec, energy_row, 0.0), axis=1, keepdims=True)
+    scale_col = lax.rsqrt(energy / MODEL_WIDTH + 1e-05) * (1.0 / math.sqrt(block))
+    exps = exps_ref[...]
+    factors = jnp.where(
+        exps >= 0, jnp.where(exps >= 1, 2.0, 1.0), jnp.where(exps >= -1, 0.5, 0.25)
+    ).astype(f32)
+    inverses = 1.0 / factors
+    blocks_each = feat // block
+    which = lax.broadcasted_iota(jnp.int32, exps.shape, 1)
+
+    def code(src):
+        for b in range(blocks_each):
+            n = src * blocks_each + b
+            pick = which == n
+            factor = jnp.sum(jnp.where(pick, factors, 0.0), axis=1, keepdims=True)
+            inverse = jnp.sum(jnp.where(pick, inverses, 0.0), axis=1, keepdims=True)
+            raw = jnp.dot(
+                hid[src, :, b * block:(b + 1) * block], table, preferred_element_type=f32
+            )
+            coded = jnp.clip(raw * scale_col * inverse, -4.0, 4.0).astype(bf16)
+            dec[src, :, b * block:(b + 1) * block] = (coded.astype(f32) * factor).astype(bf16)
+
+    code(gy)
+    for d in range(1, ny):
+        hidden_copy(d).wait()
+        code(lax.rem(gy + ny - d, ny))
+
+    def part_copy(ch, d):
+        to = lax.rem(gx + d, nx)
+        return pltpu.make_async_remote_copy(
+            src_ref=part.at[ch, to], dst_ref=got.at[ch, gx], send_sem=ps_sem.at[ch, d - 1],
+            recv_sem=pr_sem.at[ch, d - 1], device_id={"gx": to}, device_id_type=MESH,
+        )
+
+    def ship(ch, total):
+        for j in range(nx):
+            part[ch, j] = total[j * owners:(j + 1) * owners]
+        for d in range(1, nx):
+            part_copy(ch, d).start()
+
+    def project(read):
+        total = jnp.zeros((batch, CHUNK), f32)
+        for s in range(ny):
+            total = total + jnp.dot(dec[s], read(s), preferred_element_type=f32)
+        return total
+
+    ship(q_chunks, project(lambda s: kv_w[s * feat:(s + 1) * feat, :]))
+
+    def q_step(ch, carry):
+        wq_copy(ch).wait()
+        ship(ch, project(lambda s: wbuf[ch, s * feat:(s + 1) * feat, :]))
+        return carry
+
+    lax.fori_loop(0, q_chunks, q_step, 0)
+
+    wo_rows = wout_hbm.shape[0]
+    halves = depth // wo_rows
+    wo_wide = halves * CHUNK
+
+    def wo_copy(j, h):
+        return pltpu.make_async_copy(
+            wout_hbm.at[:, pl.ds(pl.multiple_of(j * wo_wide + h * CHUNK, CHUNK), CHUNK)],
+            wbuf.at[j, pl.ds(h * wo_rows, wo_rows)],
+            wo_sem.at[j, h],
+        )
+
+    for j in range(ny):
+        for h in range(halves):
+            wo_copy(j, h).start()
+
+    cosine = cos_ref[...]
+    sine = sin_ref[...]
+
+    def rope(v):
+        return v * cosine + pltpu.roll(v, head_dim // 2, 1) * sine
+
+    def arrived(ch):
+        for d in range(1, nx):
+            part_copy(ch, d).wait_recv()
+        total = part[ch, gx]
+        for d in range(1, nx):
+            total = total + got[ch, lax.rem(gx + d, nx)]
+        return total
+
+    per = CHUNK // head_dim
+    total = arrived(q_chunks)
+    for j in range(parts):
+        v = total[:, j * head_dim:(j + 1) * head_dim]
+        if j % 2 == 0:
+            v = rope(v)
+        kv2d[j * owners:(j + 1) * owners, :] = v.astype(bf16).astype(f32)
+
+    for ch in range(q_chunks):
+        total = arrived(ch)
+        for j in range(per):
+            h = ch * per + j
+            v = rope(total[:, j * head_dim:(j + 1) * head_dim])
+            q2d[h * owners:(h + 1) * owners, :] = v.astype(bf16).astype(f32)
+
+    k_copy.wait()
+    v_copy.wait()
+    factor = 1.0 / math.sqrt(head_dim)
+    position = lax.broadcasted_iota(jnp.int32, (reps, slots), 1)
+    group = 4
+
+    def attend(i, carry):
+        scores, fresh, mask, new_v = [], [], [], []
+        for jb in range(group):
+            b = i * group + jb
+            length = len_ref[b]
+            for g in range(kv_heads):
+                q = q2d[pl.ds(g * reps * owners + b, reps, stride=owners), :]
+                k_new = kv2d[pl.ds(2 * g * owners + b, 1), :]
+                new_v.append(kv2d[pl.ds((2 * g + 1) * owners + b, 1), :])
+                scores.append(
+                    lax.dot_general(
+                        q.astype(bf16), keys[b * kv_heads + g], contract,
+                        preferred_element_type=f32,
+                    )
+                )
+                fresh.append(jnp.sum(q * k_new, axis=1, keepdims=True))
+                mask.append(position < length)
+        for n in range(group * kv_heads):
+            b = i * group + n // kv_heads
+            g = n % kv_heads
+            f = fresh[n] * factor
+            s = jnp.where(mask[n], scores[n] * factor, -1e30)
+            top = jnp.maximum(jnp.max(s, axis=1, keepdims=True), f)
+            w = jnp.where(mask[n], jnp.exp(s - top), 0.0)
+            fw = jnp.exp(f - top)
+            whole = jnp.sum(w, axis=1, keepdims=True) + fw
+            probs = (w / whole).astype(bf16)
+            fp = (fw / whole).astype(bf16).astype(f32)
+            mixed = jnp.dot(probs, values[b * kv_heads + g], preferred_element_type=f32)
+            mixed = mixed + fp * new_v[n]
+            att2d[pl.ds(g * reps * owners + b, reps, stride=owners), :] = mixed
+        return carry
+
+    lax.fori_loop(0, owners // group, attend, 0)
+    for h in range(heads):
+        att_all[gx, :, h * head_dim:(h + 1) * head_dim] = att2d[
+            h * owners:(h + 1) * owners, :
+        ].astype(bf16)
+
+    def att_copy(d):
+        return pltpu.make_async_remote_copy(
+            src_ref=att_all.at[gx], dst_ref=att_all.at[gx], send_sem=as_sem.at[d - 1],
+            recv_sem=ar_sem.at[d - 1], device_id={"gx": lax.rem(gx + d, nx)}, device_id_type=MESH,
+        )
+
+    for d in range(1, nx):
+        att_copy(d).start()
+    for ch in range(q_chunks + 1):
+        for d in range(1, nx):
+            part_copy(ch, d).wait_send()
+    for j in range(ny):
+        for h in range(halves):
+            wo_copy(j, h).wait()
+    for d in range(1, nx):
+        att_copy(d).wait()
+    attended = att_all[...].reshape(batch, heads * head_dim)
+
+    def term_copy(d, h):
+        to = lax.rem(gy + d, ny)
+        return pltpu.make_async_remote_copy(
+            src_ref=term.at[to, h], dst_ref=terms_in.at[gy, h], send_sem=ts_sem.at[d - 1, h],
+            recv_sem=tr_sem.at[d - 1, h], device_id={"gy": to}, device_id_type=MESH,
+        )
+
+    def out_piece(to, h):
+        term[to, h] = jnp.dot(
+            attended, wbuf[to, h * wo_rows:(h + 1) * wo_rows, :], preferred_element_type=f32
+        )
+
+    def out_step(d, carry):
+        for h in range(halves):
+            out_piece(lax.rem(gy + d, ny), h)
+            term_copy(d, h).start()
+        return carry
+
+    lax.fori_loop(1, ny, out_step, 0)
+    for h in range(halves):
+        out_piece(gy, h)
+    for h in range(halves):
+        total = term[gy, h]
+        for d in range(1, ny):
+            term_copy(d, h).wait()
+            total = total + terms_in[lax.rem(gy + ny - d, ny), h]
+        out_ref[:, h * CHUNK:(h + 1) * CHUNK] = total.astype(bf16)
+
+
+def direct_body(
+    nx, ny, hidden_in, exponents, signs, lengths, w_query, key_value_weight, w_out,
+    keys_cache, cached_value_rows,
+):
+    batch, feat = hidden_in.shape
+    depth, q_cols = w_query.shape
+    kv_heads, head_dim = key_value_weight.shape[1], key_value_weight.shape[3]
+    owners = batch // nx
+    heads = q_cols // head_dim
+    reps = heads // kv_heads
+    slots = keys_cache.shape[2]
+    out_cols = w_out.shape[1]
+    parts = 2 * kv_heads
+    half = head_dim // 2
+    freqs = jnp.power(500000.0, -(jnp.arange(half, dtype=jnp.float32) * 2.0 / head_dim))
+    angles = lengths.astype(jnp.float32)[:, None] * freqs
+    cosine, sine = jnp.cos(angles), jnp.sin(angles)
+    cos_full = jnp.concatenate([cosine, cosine], axis=1)
+    sin_full = jnp.concatenate([-sine, sine], axis=1)
+    q_chunks = q_cols // CHUNK
+    halves = depth // w_out.shape[0]
+    dims = (batch, feat, q_cols, owners, kv_heads, reps, slots, head_dim, out_cols)
+    vmem = pl.BlockSpec(memory_space=pltpu.VMEM)
+    anyw = pl.BlockSpec(memory_space=pl.ANY)
+    f32, bf16 = jnp.float32, jnp.bfloat16
+    dma = pltpu.SemaphoreType.DMA
+    lanes = max(batch, 128)
+    return pl.pallas_call(
+        functools.partial(decode_kernel, nx, ny, dims),
+        out_shape=jax.ShapeDtypeStruct((batch, feat), bf16),
+        in_specs=[vmem] * 5 + [pl.BlockSpec(memory_space=pltpu.SMEM)] + [anyw] * 5,
+        out_specs=vmem,
+        scratch_shapes=[
+            pltpu.VMEM((q_chunks, depth, CHUNK), bf16),
+            pltpu.VMEM((depth * parts, head_dim), bf16),
+            pltpu.VMEM((1024, head_dim), f32),
+            pltpu.VMEM((depth, parts * head_dim), bf16),
+            pltpu.VMEM((owners * kv_heads, slots, head_dim), bf16),
+            pltpu.VMEM((owners * kv_heads, slots, head_dim), bf16),
+            pltpu.VMEM((ny, batch, feat), bf16),
+            pltpu.VMEM((nx * ny, 8, lanes), f32),
+            pltpu.VMEM((ny, batch, feat), bf16),
+            pltpu.VMEM((q_chunks + 1, nx, owners, CHUNK), f32),
+            pltpu.VMEM((q_chunks + 1, nx, owners, CHUNK), f32),
+            pltpu.VMEM((heads * owners, head_dim), f32),
+            pltpu.VMEM((parts * owners, head_dim), f32),
+            pltpu.VMEM((heads * owners, head_dim), f32),
+            pltpu.VMEM((nx, owners, heads * head_dim), bf16),
+            pltpu.VMEM((ny, halves, batch, CHUNK), f32),
+            pltpu.VMEM((ny, halves, batch, CHUNK), f32),
+            dma((q_chunks,)), dma, dma, dma, dma((ny, halves)),
+            dma((ny - 1,)), dma((ny - 1,)),
+            dma((nx * ny - 1,)), dma((nx * ny - 1,)),
+            dma((q_chunks + 1, nx - 1)), dma((q_chunks + 1, nx - 1)),
+            dma((nx - 1,)), dma((nx - 1,)),
+            dma((ny - 1, halves)), dma((ny - 1, halves)),
+        ],
+        compiler_params=pltpu.CompilerParams(
+            collective_id=0, has_side_effects=True, vmem_limit_bytes=56 * 1024 * 1024
+        ),
+    )(
+        hidden_in, exponents, signs.reshape(1, -1), cos_full, sin_full, lengths,
+        w_query, key_value_weight.reshape(-1, head_dim), w_out,
+        keys_cache.reshape(-1, slots, head_dim), cached_value_rows.reshape(-1, slots, head_dim),
+    )
 
 
 def hadamard_table(block_len):
@@ -138,4 +524,6 @@
         P(("group", "gx"), "gy", None, None),
     )
     out_specs = P("group", ("gx", "gy"))
-    return jax.shard_map(body, mesh=mesh, in_specs=in_specs, out_specs=out_specs, check_vma=False)
+    nx, ny = mesh.shape["gx"], mesh.shape["gy"]
+    run = functools.partial(direct_body, nx, ny) if nx * ny <= 16 else body
+    return jax.shard_map(run, mesh=mesh, in_specs=in_specs, out_specs=out_specs, check_vma=False)

time: 171 us -> 59.9 us (0.35)
  blocking collectives: 55.2 us -> 0 us
  Pallas kernels: 0 us -> 54.3 us
  waiting for transfers between devices: 50.4 us -> 0 us
  matrix products: 32.8 us -> 0 us
  between operations: 13.6 us -> 0.02 us
  other arithmetic: 6.87 us -> 1.46 us
  local copies, waits for them, and re-layouts: 7.51 us -> 2.98 us
  starting transfers between devices: 3.39 us -> 0 us
    pallas_call x0 -> x1, Pallas kernels: none -> 54.3 us  [direct_body(): pl.pallas_call(functools.partial(decode_kernel, nx, ny, dims), out_shape=...]
    reduce_scatter x2 -> x0, waiting for transfers between devices: 44.6 us -> none  [the longest x1 24.5 us: body(): summed = lax.psum_scatter(terms, 'gy', scatter_dimension=1, tiled=True)]
    psum x1 -> x0, blocking collectives: 34.9 us -> none  [body(): lax.psum(jnp.sum(widened * widened, axis=1, keepdims=True), ('gx', 'gy'))]
    dot_general x7 -> x0, matrix products: 32.8 us -> none  [the longest x1 9.79 us: body(): jnp.dot(lax.all_gather(attended, 'gx', axis=0, tiled=True), w_out, prefer...]
    all_gather x2 -> x0, blocking collectives: 20.3 us -> none  [the longest x1 13.8 us: body(): lax.all_gather(attended, 'gx', axis=0, tiled=True)]
    reshape x2 -> x0, local copies, waits for them, and re-layouts: 7.23 us -> none  [the longest x1 7.21 us: body(): key_value_weight.reshape(key_value_weight.shape[0], kv_heads * 2 * head_dim)]
    all_to_all x1 -> x0, waiting for transfers between devices: 5.78 us -> none  [body(): lax.all_to_all(partial_cols, 'gx', split_axis=0, concat_axis=1, tiled=True)]
    all_to_all x1 -> x0, starting transfers between devices: 3.34 us -> none  [body(): lax.all_to_all(partial_cols, 'gx', split_axis=0, concat_axis=1, tiled=True)]
  transfers between devices with their start and end apart: 3 -> 0, of which waited for: 3 -> 0; matrix products, arithmetic and copies ran while one was open for 0% -> 0% of each run, Pallas kernels for 0% -> 0%
where the time goes in v1:
time: 59.9 us; the launch traced here: 58.8 us
  Pallas kernels  54.3 us (91%)
  local copies, waits for them, and re-layouts  2.98 us (5%)
  other arithmetic  1.46 us (2%)
    pallas_call x1, Pallas kernels, direct_body(): pl.pallas_call(functools.partial(decode_kernel, nx, ny, dims), out_shape=...  54.3 us
    unnamed x2, local copies, waits for them, and re-layouts  2.98 us

profile of v1, /device:TPU:0, one launch (start us, length us, event | category | flops | bytes accessed | tf_op | source)
XLA Modules:
  0.0 58.8 jit_solution(12366053478311432560)
XLA Ops:
  0.0 0.7 %convert_element_type.3 = f32[16]{0:T(128)S(1)} convert(s32[16]{0:T(128)} %len_ref.1) | non-fusion elementwise | flops 16 | bytes 128 | tf_op jit(solution)/shard_map/convert_element_type | solution.py:345
  0.7 0.1 fusion
  0.8 0.7 %pad_maximum_fusion = (f32[16,128]{1,0:T(8,128)}, f32[16,128]{1,0:T(8,128)}) fusion(f32[16,64]{1,0:T(8,128)S(1)} %get-tuple-element.7, f32[16,64]{1,0:T(8,128)S(1)} %get-tuple-element.6, f32[16,64]{1,0:T(8,128)S(1)} %get-tuple-element.5), kind=kLoop, calls=%fused_computation.2 | loop fusion | flops 4096 | bytes 28672 | tf_op jit(solution)/shard_map/concatenate | solution.py:347
  1.5 1.4 %copy.10.exps_ref = s32[64,32]{1,0:T(8,128)} copy(s32[64,32]{0,1:T(8,128)} %param.10) | data formatting | bytes 16384 | tf_op args[1]
  2.9 54.3 %shard_map.91 = bf16[64,1024]{1,0:T(8,128)(2,1)} custom-call(bf16[64,1024]{1,0:T(8,128)(2,1)} %hidden_ref.1, s32[64,32]{1,0:T(8,128)} %copy.10.exps_ref, s32[1,128]{1,0:T(1,128)} %bitcast.7, f32[16,128]{1,0:T(8,128)} %get-tuple-element.8.cos_ref, f32[16,128]{1,0:T(8,128)} %get-tuple-element.9.sin_ref, s32[16]{0:T(128)} %len_ref.1, ...), custom_call_target="tpu_custom_call" | custom-call | tf_op jit(solution)/shard_map/pallas_call | solution.py:357
  57.2 1.6 %copy.12 = bf16[64,1024]{1,0:T(8,128)(2,1)} copy(bf16[64,1024]{1,0:T(8,128)(2,1)} %shard_map.91) | data formatting | bytes 262144
  (1 shorter events, 0.0 us)

commit v2 on v1

--- a/solution.py
+++ b/solution.py
@@ -3,6 +3,7 @@
 
 import jax
 import jax.numpy as jnp
+import numpy as np
 from jax import lax
 from jax.experimental import pallas as pl
 from jax.experimental.pallas import tpu as pltpu
@@ -15,18 +16,22 @@
 
 def decode_kernel(
     nx, ny, dims,
-    hidden_ref, exps_ref, signs_ref, cos_ref, sin_ref, len_ref,
+    hidden_ref, exps_ref, signs_ref, freq_ref, len_row_ref, len_ref,
     wq_hbm, kv_hbm, wout_hbm, keys_hbm, values_hbm,
     out_ref,
     wbuf, kv_raw, kv_stage, kv_w, keys, values,
-    hid, en, dec, part, got, q2d, kv2d, att2d, att_all, term, terms_in,
+    hid, en, dec, part, got, q2d, kv2d, att2d, att_all, term, pair_in, cross_in,
     w_sem, kv_sem, k_sem, v_sem, wo_sem,
-    hs_sem, hr_sem, es_sem, er_sem, ps_sem, pr_sem, as_sem, ar_sem, ts_sem, tr_sem,
+    hs_sem, hr_sem, es_sem, er_sem, ps_sem, pr_sem, as_sem, ar_sem,
+    ts_sem, tr_sem, xs_sem, xr_sem,
 ):
     batch, feat, q_cols, owners, kv_heads, reps, slots, head_dim, out_cols = dims
     gx = lax.axis_index("gx")
     gy = lax.axis_index("gy")
     peers = nx * ny
+    chips = ny // 2
+    chip, core = gy // 2, lax.rem(gy, 2)
+    buddy = chip * 2 + 1 - core
     me = gx * ny + gy
     block = head_dim
     q_chunks = q_cols // CHUNK
@@ -90,16 +95,31 @@
         energy_copy(k).start()
         return carry
 
+    def across(e):
+        return lax.rem(chip + e, chips) * 2 + core
+
+    def hidden_copy(n):
+        src = gy if n < chips else lax.rem(chip + chips - (n - chips + 1), chips) * 2 + core
+        to = across(n) if 1 <= n < chips else buddy
+        return pltpu.make_async_remote_copy(
+            src_ref=hid.at[src], dst_ref=hid.at[src], send_sem=hs_sem.at[n],
+            recv_sem=hr_sem.at[n], device_id={"gy": to}, device_id_type=MESH,
+        )
+
+    for e in range(1, chips):
+        hidden_copy(e).start()
     lax.fori_loop(1, peers, send_energy, 0)
-
-    def hidden_copy(d):
-        return pltpu.make_async_remote_copy(
-            src_ref=hid.at[gy], dst_ref=hid.at[gy], send_sem=hs_sem.at[d - 1],
-            recv_sem=hr_sem.at[d - 1], device_id={"gy": lax.rem(gy + d, ny)}, device_id_type=MESH,
-        )
-
-    for d in range(1, ny):
-        hidden_copy(d).start()
+    hidden_copy(0).start()
+
+    lr = lax.broadcasted_iota(jnp.int32, (owners, owners), 0)
+    lc = lax.broadcasted_iota(jnp.int32, (owners, owners), 1)
+    place = jnp.sum(
+        jnp.where(lr == lc, len_row_ref[...].astype(f32), 0.0), axis=1, keepdims=True
+    )
+    angles = place * freq_ref[...]
+    first = lax.broadcasted_iota(jnp.int32, (owners, head_dim), 1) < head_dim // 2
+    cosine = jnp.cos(angles)
+    sine = jnp.where(first, -1.0, 1.0) * jnp.sin(angles)
 
     kv_copy().wait()
     parts = kv_heads * 2
@@ -128,6 +148,10 @@
     sign_col = jnp.sum(jnp.where(r == c, sign_row, 0.0), axis=1, keepdims=True)
     table = (jnp.where((parity & 1) == 0, 1.0, -1.0) * sign_col).astype(bf16)
 
+    for e in range(1, chips):
+        hidden_copy(e).wait_recv()
+        hidden_copy(chips - 1 + e).start()
+
     def wait_energy(k, carry):
         energy_copy(k).wait()
         return carry
@@ -138,20 +162,20 @@
     ec = lax.broadcasted_iota(jnp.int32, (batch, lanes), 1)
     energy = jnp.sum(jnp.where(er == ec, energy_row, 0.0), axis=1, keepdims=True)
     scale_col = lax.rsqrt(energy / MODEL_WIDTH + 1e-05) * (1.0 / math.sqrt(block))
-    exps = exps_ref[...]
-    factors = jnp.where(
-        exps >= 0, jnp.where(exps >= 1, 2.0, 1.0), jnp.where(exps >= -1, 0.5, 0.25)
-    ).astype(f32)
-    inverses = 1.0 / factors
     blocks_each = feat // block
-    which = lax.broadcasted_iota(jnp.int32, exps.shape, 1)
+    own_lane = lax.broadcasted_iota(jnp.int32, (batch, batch), 0) == lax.broadcasted_iota(
+        jnp.int32, (batch, batch), 1
+    )
 
     def code(src):
         for b in range(blocks_each):
             n = src * blocks_each + b
-            pick = which == n
-            factor = jnp.sum(jnp.where(pick, factors, 0.0), axis=1, keepdims=True)
-            inverse = jnp.sum(jnp.where(pick, inverses, 0.0), axis=1, keepdims=True)
+            exps = exps_ref[pl.ds(n, 1), :]
+            factors = jnp.where(
+                exps >= 0, jnp.where(exps >= 1, 2.0, 1.0), jnp.where(exps >= -1, 0.5, 0.25)
+            )
+            factor = jnp.sum(jnp.where(own_lane, factors, 0.0), axis=1, keepdims=True)
+            inverse = 1.0 / factor
             raw = jnp.dot(
                 hid[src, :, b * block:(b + 1) * block], table, preferred_element_type=f32
             )
@@ -159,9 +183,15 @@
             dec[src, :, b * block:(b + 1) * block] = (coded.astype(f32) * factor).astype(bf16)
 
     code(gy)
-    for d in range(1, ny):
-        hidden_copy(d).wait()
-        code(lax.rem(gy + ny - d, ny))
+    for e in range(1, chips):
+        code(lax.rem(chip + chips - e, chips) * 2 + core)
+    hidden_copy(0).wait_recv()
+    code(buddy)
+    for e in range(1, chips):
+        hidden_copy(chips - 1 + e).wait_recv()
+        code(lax.rem(chip + chips - e, chips) * 2 + 1 - core)
+    for n in range(ny - 1):
+        hidden_copy(n).wait_send()
 
     def part_copy(ch, d):
         to = lax.rem(gx + d, nx)
@@ -205,9 +235,6 @@
     for j in range(ny):
         for h in range(halves):
             wo_copy(j, h).start()
-
-    cosine = cos_ref[...]
-    sine = sin_ref[...]
 
     def rope(v):
         return v * cosine + pltpu.roll(v, head_dim // 2, 1) * sine
@@ -239,28 +266,24 @@
     v_copy.wait()
     factor = 1.0 / math.sqrt(head_dim)
     position = lax.broadcasted_iota(jnp.int32, (reps, slots), 1)
-    group = 4
-
-    def attend(i, carry):
+    group = 8
+
+    def attend(g, i, carry):
         scores, fresh, mask, new_v = [], [], [], []
         for jb in range(group):
             b = i * group + jb
-            length = len_ref[b]
-            for g in range(kv_heads):
-                q = q2d[pl.ds(g * reps * owners + b, reps, stride=owners), :]
-                k_new = kv2d[pl.ds(2 * g * owners + b, 1), :]
-                new_v.append(kv2d[pl.ds((2 * g + 1) * owners + b, 1), :])
-                scores.append(
-                    lax.dot_general(
-                        q.astype(bf16), keys[b * kv_heads + g], contract,
-                        preferred_element_type=f32,
-                    )
+            q = q2d[pl.ds(g * reps * owners + b, reps, stride=owners), :]
+            k_new = kv2d[pl.ds(2 * g * owners + b, 1), :]
+            new_v.append(kv2d[pl.ds((2 * g + 1) * owners + b, 1), :])
+            scores.append(
+                lax.dot_general(
+                    q.astype(bf16), keys[b * kv_heads + g], contract, preferred_element_type=f32
                 )
-                fresh.append(jnp.sum(q * k_new, axis=1, keepdims=True))
-                mask.append(position < length)
-        for n in range(group * kv_heads):
-            b = i * group + n // kv_heads
-            g = n % kv_heads
+            )
+            fresh.append(jnp.sum(q * k_new, axis=1, keepdims=True))
+            mask.append(position < len_ref[b])
+        for n in range(group):
+            b = i * group + n
             f = fresh[n] * factor
             s = jnp.where(mask[n], scores[n] * factor, -1e30)
             top = jnp.maximum(jnp.max(s, axis=1, keepdims=True), f)
@@ -274,57 +297,80 @@
             att2d[pl.ds(g * reps * owners + b, reps, stride=owners), :] = mixed
         return carry
 
-    lax.fori_loop(0, owners // group, attend, 0)
-    for h in range(heads):
-        att_all[gx, :, h * head_dim:(h + 1) * head_dim] = att2d[
-            h * owners:(h + 1) * owners, :
-        ].astype(bf16)
-
-    def att_copy(d):
+    def att_copy(g, d):
         return pltpu.make_async_remote_copy(
-            src_ref=att_all.at[gx], dst_ref=att_all.at[gx], send_sem=as_sem.at[d - 1],
-            recv_sem=ar_sem.at[d - 1], device_id={"gx": lax.rem(gx + d, nx)}, device_id_type=MESH,
-        )
-
-    for d in range(1, nx):
-        att_copy(d).start()
+            src_ref=att_all.at[g, gx], dst_ref=att_all.at[g, gx], send_sem=as_sem.at[g, d - 1],
+            recv_sem=ar_sem.at[g, d - 1], device_id={"gx": lax.rem(gx + d, nx)},
+            device_id_type=MESH,
+        )
+
+    for g in range(kv_heads):
+        lax.fori_loop(0, owners // group, functools.partial(attend, g), 0)
+        for h in range(reps):
+            at = (g * reps + h) * owners
+            att_all[g, gx, :, h * head_dim:(h + 1) * head_dim] = att2d[
+                at:at + owners, :
+            ].astype(bf16)
+        for d in range(1, nx):
+            att_copy(g, d).start()
     for ch in range(q_chunks + 1):
         for d in range(1, nx):
             part_copy(ch, d).wait_send()
     for j in range(ny):
         for h in range(halves):
             wo_copy(j, h).wait()
-    for d in range(1, nx):
-        att_copy(d).wait()
-    attended = att_all[...].reshape(batch, heads * head_dim)
-
-    def term_copy(d, h):
-        to = lax.rem(gy + d, ny)
+    for g in range(kv_heads):
+        for d in range(1, nx):
+            att_copy(g, d).wait()
+    width = reps * head_dim
+    attended = [att_all[g].reshape(batch, width) for g in range(kv_heads)]
+
+    def pair_copy(e, h):
         return pltpu.make_async_remote_copy(
-            src_ref=term.at[to, h], dst_ref=terms_in.at[gy, h], send_sem=ts_sem.at[d - 1, h],
-            recv_sem=tr_sem.at[d - 1, h], device_id={"gy": to}, device_id_type=MESH,
+            src_ref=term.at[e, 0, h], dst_ref=pair_in.at[e, h], send_sem=ts_sem.at[e, h],
+            recv_sem=tr_sem.at[e, h], device_id={"gy": buddy}, device_id_type=MESH,
+        )
+
+    def cross_copy(e, h):
+        return pltpu.make_async_remote_copy(
+            src_ref=term.at[e, 1, h], dst_ref=cross_in.at[e - 1, h], send_sem=xs_sem.at[e - 1, h],
+            recv_sem=xr_sem.at[e - 1, h], device_id={"gy": across(e)}, device_id_type=MESH,
         )
 
     def out_piece(to, h):
-        term[to, h] = jnp.dot(
-            attended, wbuf[to, h * wo_rows:(h + 1) * wo_rows, :], preferred_element_type=f32
-        )
-
-    def out_step(d, carry):
+        total = jnp.zeros((batch, CHUNK), f32)
+        for g in range(kv_heads):
+            at = h * wo_rows + g * width
+            total = total + jnp.dot(
+                attended[g], wbuf[to, at:at + width, :], preferred_element_type=f32
+            )
+        return total
+
+    for e in list(range(1, chips)) + [0]:
+        there = lax.rem(chip + e, chips) * 2
         for h in range(halves):
-            out_piece(lax.rem(gy + d, ny), h)
-            term_copy(d, h).start()
-        return carry
-
-    lax.fori_loop(1, ny, out_step, 0)
+            term[e, 0, h] = out_piece(there + 1 - core, h)
+            pair_copy(e, h).start()
+        for h in range(halves):
+            total = out_piece(there + core, h)
+            if e > 0:
+                pair_copy(e, h).wait_recv()
+                term[e, 1, h] = total + pair_in[e, h]
+                cross_copy(e, h).start()
+            else:
+                term[e, 1, h] = total
     for h in range(halves):
-        out_piece(gy, h)
+        pair_copy(0, h).wait_recv()
+        total = term[0, 1, h] + pair_in[0, h]
+        for e in range(1, chips):
+            cross_copy(e, h).wait_recv()
+            total = total + cross_in[e - 1, h]
+        out_ref[:, h * CHUNK:(h + 1) * CHUNK] = total.astype(bf16)
     for h in range(halves):
-        total = term[gy, h]
-        for d in range(1, ny):
-            term_copy(d, h).wait()
-            total = total + terms_in[lax.rem(gy + ny - d, ny), h]
-        out_ref[:, h * CHUNK:(h + 1) * CHUNK] = total.astype(bf16)
+        for e in range(chips):
+            pair_copy(e, h).wait_send()
+        for e in range(1, chips):
+            cross_copy(e, h).wait_send()
 
 
 def direct_body(
@@ -341,13 +387,11 @@
     out_cols = w_out.shape[1]
     parts = 2 * kv_heads
     half = head_dim // 2
-    freqs = jnp.power(500000.0, -(jnp.arange(half, dtype=jnp.float32) * 2.0 / head_dim))
-    angles = lengths.astype(jnp.float32)[:, None] * freqs
-    cosine, sine = jnp.cos(angles), jnp.sin(angles)
-    cos_full = jnp.concatenate([cosine, cosine], axis=1)
-    sin_full = jnp.concatenate([-sine, sine], axis=1)
+    freqs = np.power(500000.0, -(np.arange(half) * 2.0 / head_dim)).astype(np.float32)
+    freqs = jnp.asarray(np.concatenate([freqs, freqs])[None, :])
     q_chunks = q_cols // CHUNK
     halves = depth // w_out.shape[0]
+    chips = ny // 2
     dims = (batch, feat, q_cols, owners, kv_heads, reps, slots, head_dim, out_cols)
     vmem = pl.BlockSpec(memory_space=pltpu.VMEM)
     anyw = pl.BlockSpec(memory_space=pl.ANY)
@@ -374,21 +418,23 @@
             pltpu.VMEM((heads * owners, head_dim), f32),
             pltpu.VMEM((parts * owners, head_dim), f32),
             pltpu.VMEM((heads * owners, head_dim), f32),
-            pltpu.VMEM((nx, owners, heads * head_dim), bf16),
-            pltpu.VMEM((ny, halves, batch, CHUNK), f32),
-            pltpu.VMEM((ny, halves, batch, CHUNK), f32),
+            pltpu.VMEM((kv_heads, nx, owners, reps * head_dim), bf16),
+            pltpu.VMEM((chips, 2, halves, batch, CHUNK), f32),
+            pltpu.VMEM((chips, halves, batch, CHUNK), f32),
+            pltpu.VMEM((chips - 1, halves, batch, CHUNK), f32),
             dma((q_chunks,)), dma, dma, dma, dma((ny, halves)),
             dma((ny - 1,)), dma((ny - 1,)),
             dma((nx * ny - 1,)), dma((nx * ny - 1,)),
             dma((q_chunks + 1, nx - 1)), dma((q_chunks + 1, nx - 1)),
-            dma((nx - 1,)), dma((nx - 1,)),
-            dma((ny - 1, halves)), dma((ny - 1, halves)),
+            dma((kv_heads, nx - 1)), dma((kv_heads, nx - 1)),
+            dma((chips, halves)), dma((chips, halves)),
+            dma((chips - 1, halves)), dma((chips - 1, halves)),
         ],
         compiler_params=pltpu.CompilerParams(
             collective_id=0, has_side_effects=True, vmem_limit_bytes=56 * 1024 * 1024
         ),
     )(
-        hidden_in, exponents, signs.reshape(1, -1), cos_full, sin_full, lengths,
+        hidden_in, exponents.T, signs.reshape(1, -1), freqs, lengths.reshape(1, -1), lengths,
         w_query, key_value_weight.reshape(-1, head_dim), w_out,
         keys_cache.reshape(-1, slots, head_dim), cached_value_rows.reshape(-1, slots, head_dim),
     )

time: 59.9 us -> 51.7 us (0.86); the launches traced: 58.8 us -> 51.5 us
  Pallas kernels: 54.3 us -> 50 us
  other arithmetic: 1.46 us -> 0 us
  local copies, waits for them, and re-layouts: 2.98 us -> 1.57 us
    pallas_call x1, Pallas kernels: 54.3 us -> 50 us  [direct_body(): pl.pallas_call(functools.partial(decode_kernel, nx, ny, dims), out_shape=...]
    unnamed x2 -> x1, local copies, waits for them, and re-layouts: 2.98 us -> 1.57 us
    concatenate x1 -> x0, other arithmetic: 0.67 us -> none  [direct_body(): cos_full = jnp.concatenate([cosine, cosine], axis=1)]
    convert_element_type x1 -> x0, other arithmetic: 0.66 us -> none  [direct_body(): angles = lengths.astype(jnp.float32)[:, None] * freqs]
where the time goes in v2:
time: 51.7 us; the launch traced here: 51.5 us
  Pallas kernels  50 us (97%)
  local copies, waits for them, and re-layouts  1.57 us (3%)
    pallas_call x1, Pallas kernels, direct_body(): pl.pallas_call(functools.partial(decode_kernel, nx, ny, dims), out_shape=...  50 us
    unnamed x1, local copies, waits for them, and re-layouts  1.57 us

profile of v2, /device:TPU:0, one launch (start us, length us, event | category | flops | bytes accessed | tf_op | source)
XLA Modules:
  0.0 51.5 jit_solution(17530045767049678470)
XLA Ops:
  0.0 50.0 %shard_map.100 = bf16[64,1024]{1,0:T(8,128)(2,1)} custom-call(bf16[64,1024]{1,0:T(8,128)(2,1)} %hidden_ref.1, s32[32,64]{1,0:T(8,128)} %bitcast.9, s32[1,128]{1,0:T(1,128)} %bitcast.11, f32[1,128]{1,0:T(1,128)} %constant.2.clone.freq_ref, s32[1,16]{1,0:T(1,128)} %bitcast.10, s32[16]{0:T(128)} %len_ref.1, bf16[4096,2048]{1,0:T(8,128)(2,1)} %wq_hbm.1, ...), custom_call_target="tpu_custom_call" | custom-call | tf_op jit(solution)/shard_map/pallas_call | solution.py:401
  50.0 1.6 %copy.12 = bf16[64,1024]{1,0:T(8,128)(2,1)} copy(bf16[64,1024]{1,0:T(8,128)(2,1)} %shard_map.100) | data formatting | bytes 262144

commit v3 on v2

--- a/solution.py
+++ b/solution.py
@@ -39,6 +39,18 @@
     heads = kv_heads * reps
     f32, bf16 = jnp.float32, jnp.bfloat16
 
+    barrier = pltpu.get_barrier_semaphore()
+
+    def peer(k):
+        idx = lax.rem(me + k, peers)
+        return {"gx": idx // ny, "gy": lax.rem(idx, ny)}
+
+    def greet(k, carry):
+        pl.semaphore_signal(barrier, inc=1, device_id=peer(k), device_id_type=MESH)
+        return carry
+
+    lax.fori_loop(1, peers, greet, 0)
+
     def kv_copy():
         return pltpu.make_async_copy(kv_hbm, kv_raw, kv_sem)
 
@@ -52,20 +64,6 @@
         wq_copy(c).start()
     k_copy = pltpu.make_async_copy(keys_hbm, keys, k_sem)
     v_copy = pltpu.make_async_copy(values_hbm, values, v_sem)
-    k_copy.start()
-    v_copy.start()
-
-    barrier = pltpu.get_barrier_semaphore()
-
-    def peer(k):
-        idx = lax.rem(me + k, peers)
-        return {"gx": idx // ny, "gy": lax.rem(idx, ny)}
-
-    def greet(k, carry):
-        pl.semaphore_signal(barrier, inc=1, device_id=peer(k), device_id_type=MESH)
-        return carry
-
-    lax.fori_loop(1, peers, greet, 0)
 
     own = hidden_ref[...]
     wide = own.astype(f32)
@@ -162,6 +160,8 @@
     ec = lax.broadcasted_iota(jnp.int32, (batch, lanes), 1)
     energy = jnp.sum(jnp.where(er == ec, energy_row, 0.0), axis=1, keepdims=True)
     scale_col = lax.rsqrt(energy / MODEL_WIDTH + 1e-05) * (1.0 / math.sqrt(block))
+    k_copy.start()
+    v_copy.start()
     blocks_each = feat // block
     own_lane = lax.broadcasted_iota(jnp.int32, (batch, batch), 0) == lax.broadcasted_iota(
         jnp.int32, (batch, batch), 1
@@ -255,13 +255,14 @@
             v = rope(v)
         kv2d[j * owners:(j + 1) * owners, :] = v.astype(bf16).astype(f32)
 
-    for ch in range(q_chunks):
+    def take(ch):
         total = arrived(ch)
         for j in range(per):
             h = ch * per + j
             v = rope(total[:, j * head_dim:(j + 1) * head_dim])
             q2d[h * owners:(h + 1) * owners, :] = v.astype(bf16).astype(f32)
 
+    taken = 0
     k_copy.wait()
     v_copy.wait()
     factor = 1.0 / math.sqrt(head_dim)
@@ -305,6 +306,9 @@
         )
 
     for g in range(kv_heads):
+        while taken < q_chunks and taken * per < (g + 1) * reps:
+            take(taken)
+            taken += 1
         lax.fori_loop(0, owners // group, functools.partial(attend, g), 0)
         for h in range(reps):
             at = (g * reps + h) * owners
@@ -319,11 +323,32 @@
     for j in range(ny):
         for h in range(halves):
             wo_copy(j, h).wait()
+    width = reps * head_dim
+
+    def out_piece(to, h, g):
+        at = h * wo_rows + g * width
+        return jnp.dot(
+            att_all[g].reshape(batch, width), wbuf[to, at:at + width, :],
+            preferred_element_type=f32,
+        )
+
+    def place_of(e, role):
+        return lax.rem(chip + e, chips) * 2 + (core if role else 1 - core)
+
     for g in range(kv_heads):
         for d in range(1, nx):
             att_copy(g, d).wait()
-    width = reps * head_dim
-    attended = [att_all[g].reshape(batch, width) for g in range(kv_heads)]
+        if g == kv_heads - 1:
+            break
+        for e in range(chips):
+            for role in range(2):
+                for h in range(halves):
+                    piece = out_piece(place_of(e, role), h, g)
+                    term[e, role, h] = piece if g == 0 else term[e, role, h] + piece
+
+    def finish(e, role, h):
+        piece = out_piece(place_of(e, role), h, kv_heads - 1)
+        return piece if kv_heads == 1 else term[e, role, h] + piece
 
     def pair_copy(e, h):
         return pltpu.make_async_remote_copy(
@@ -337,22 +362,12 @@
             recv_sem=xr_sem.at[e - 1, h], device_id={"gy": across(e)}, device_id_type=MESH,
         )
 
-    def out_piece(to, h):
-        total = jnp.zeros((batch, CHUNK), f32)
-        for g in range(kv_heads):
-            at = h * wo_rows + g * width
-            total = total + jnp.dot(
-                attended[g], wbuf[to, at:at + width, :], preferred_element_type=f32
-            )
-        return total
-
     for e in list(range(1, chips)) + [0]:
-        there = lax.rem(chip + e, chips) * 2
         for h in range(halves):
-            term[e, 0, h] = out_piece(there + 1 - core, h)
+            term[e, 0, h] = finish(e, 0, h)
             pair_copy(e, h).start()
         for h in range(halves):
-            total = out_piece(there + core, h)
+            total = finish(e, 1, h)
             if e > 0:
                 pair_copy(e, h).wait_recv()
                 term[e, 1, h] = total + pair_in[e, h]

time: 51.7 us -> 49.3 us (0.954)
  Pallas kernels: 50 us -> 47.6 us
    pallas_call x1, Pallas kernels: 50 us -> 47.6 us  [direct_body(): pl.pallas_call(functools.partial(decode_kernel, nx, ny, dims), out_shape=...]
where the time goes in v3:
time: 49.3 us; the launch traced here: 49.2 us
  Pallas kernels  47.6 us (97%)
  local copies, waits for them, and re-layouts  1.57 us (3%)
    pallas_call x1, Pallas kernels, direct_body(): pl.pallas_call(functools.partial(decode_kernel, nx, ny, dims), out_shape=...  47.6 us
    unnamed x1, local copies, waits for them, and re-layouts  1.57 us

profile of v3, /device:TPU:0, one launch (start us, length us, event | category | flops | bytes accessed | tf_op | source)
XLA Modules:
  0.0 49.2 jit_solution(15351433634340789077)
XLA Ops:
  0.0 47.6 %shard_map.100 = bf16[64,1024]{1,0:T(8,128)(2,1)} custom-call(bf16[64,1024]{1,0:T(8,128)(2,1)} %hidden_ref.1, s32[32,64]{1,0:T(8,128)} %bitcast.9, s32[1,128]{1,0:T(1,128)} %bitcast.11, f32[1,128]{1,0:T(1,128)} %constant.2.clone.freq_ref, s32[1,16]{1,0:T(1,128)} %bitcast.10, s32[16]{0:T(128)} %len_ref.1, bf16[4096,2048]{1,0:T(8,128)(2,1)} %wq_hbm.1, ...), custom_call_target="tpu_custom_call" | custom-call | tf_op jit(solution)/shard_map/pallas_call | solution.py:416
  47.6 1.6 %copy.12 = bf16[64,1024]{1,0:T(8,128)(2,1)} copy(bf16[64,1024]{1,0:T(8,128)(2,1)} %shard_map.100) | data formatting | bytes 262144

commit v4 on v3

--- a/solution.py
+++ b/solution.py
@@ -20,7 +20,7 @@
     wq_hbm, kv_hbm, wout_hbm, keys_hbm, values_hbm,
     out_ref,
     wbuf, kv_raw, kv_stage, kv_w, keys, values,
-    hid, en, dec, part, got, q2d, kv2d, att2d, att_all, term, pair_in, cross_in,
+    hid, en, scales, dec, part, got, q2d, kv2d, att2d, att_all, term, pair_in, cross_in,
     w_sem, kv_sem, k_sem, v_sem, wo_sem,
     hs_sem, hr_sem, es_sem, er_sem, ps_sem, pr_sem, as_sem, ar_sem,
     ts_sem, tr_sem, xs_sem, xr_sem,
@@ -59,8 +59,11 @@
             wq_hbm.at[:, pl.ds(pl.multiple_of(c * CHUNK, CHUNK), CHUNK)], wbuf.at[c], w_sem.at[c]
         )
 
+    early = min(q_chunks, -(-reps * head_dim // CHUNK))
+    for c in range(early):
+        wq_copy(c).start()
     kv_copy().start()
-    for c in range(q_chunks):
+    for c in range(early, q_chunks):
         wq_copy(c).start()
     k_copy = pltpu.make_async_copy(keys_hbm, keys, k_sem)
     v_copy = pltpu.make_async_copy(values_hbm, values, v_sem)
@@ -119,23 +122,6 @@
     cosine = jnp.cos(angles)
     sine = jnp.where(first, -1.0, 1.0) * jnp.sin(angles)
 
-    kv_copy().wait()
-    parts = kv_heads * 2
-    step_rows = kv_stage.shape[0]
-    rows_out = step_rows // parts
-
-    def separate(i, carry):
-        base = pl.multiple_of(i * step_rows, step_rows)
-        kv_stage[...] = kv_raw[pl.ds(base, step_rows), :].astype(f32)
-        to = pl.multiple_of(i * rows_out, rows_out)
-        for j in range(parts):
-            kv_w[pl.ds(to, rows_out), j * head_dim:(j + 1) * head_dim] = kv_stage[
-                pl.ds(j, rows_out, stride=parts), :
-            ].astype(bf16)
-        return carry
-
-    lax.fori_loop(0, depth // rows_out, separate, 0)
-
     r = lax.broadcasted_iota(jnp.int32, (block, block), 0)
     c = lax.broadcasted_iota(jnp.int32, (block, block), 1)
     common = r & c
@@ -146,6 +132,22 @@
     sign_col = jnp.sum(jnp.where(r == c, sign_row, 0.0), axis=1, keepdims=True)
     table = (jnp.where((parity & 1) == 0, 1.0, -1.0) * sign_col).astype(bf16)
 
+    own_lane = lax.broadcasted_iota(jnp.int32, (batch, batch), 0) == lax.broadcasted_iota(
+        jnp.int32, (batch, batch), 1
+    )
+
+    def spread(n, carry):
+        exps = exps_ref[pl.ds(n, 1), :]
+        factors = jnp.where(
+            exps >= 0, jnp.where(exps >= 1, 2.0, 1.0), jnp.where(exps >= -1, 0.5, 0.25)
+        )
+        factor = jnp.sum(jnp.where(own_lane, factors, 0.0), axis=1, keepdims=True)
+        scales[n, 0] = jnp.broadcast_to(factor, (batch, block))
+        scales[n, 1] = jnp.broadcast_to(1.0 / factor, (batch, block))
+        return carry
+
+    lax.fori_loop(0, depth // block, spread, 0)
+
     for e in range(1, chips):
         hidden_copy(e).wait_recv()
         hidden_copy(chips - 1 + e).start()
@@ -163,24 +165,14 @@
     k_copy.start()
     v_copy.start()
     blocks_each = feat // block
-    own_lane = lax.broadcasted_iota(jnp.int32, (batch, batch), 0) == lax.broadcasted_iota(
-        jnp.int32, (batch, batch), 1
-    )
-
     def code(src):
         for b in range(blocks_each):
             n = src * blocks_each + b
-            exps = exps_ref[pl.ds(n, 1), :]
-            factors = jnp.where(
-                exps >= 0, jnp.where(exps >= 1, 2.0, 1.0), jnp.where(exps >= -1, 0.5, 0.25)
-            )
-            factor = jnp.sum(jnp.where(own_lane, factors, 0.0), axis=1, keepdims=True)
-            inverse = 1.0 / factor
             raw = jnp.dot(
                 hid[src, :, b * block:(b + 1) * block], table, preferred_element_type=f32
             )
-            coded = jnp.clip(raw * scale_col * inverse, -4.0, 4.0).astype(bf16)
-            dec[src, :, b * block:(b + 1) * block] = (coded.astype(f32) * factor).astype(bf16)
+            coded = jnp.clip(raw * scale_col * scales[n, 1], -4.0, 4.0).astype(bf16)
+            dec[src, :, b * block:(b + 1) * block] = (coded.astype(f32) * scales[n, 0]).astype(bf16)
 
     code(gy)
     for e in range(1, chips):
@@ -212,14 +204,31 @@
             total = total + jnp.dot(dec[s], read(s), preferred_element_type=f32)
         return total
 
-    ship(q_chunks, project(lambda s: kv_w[s * feat:(s + 1) * feat, :]))
-
     def q_step(ch, carry):
         wq_copy(ch).wait()
         ship(ch, project(lambda s: wbuf[ch, s * feat:(s + 1) * feat, :]))
         return carry
 
-    lax.fori_loop(0, q_chunks, q_step, 0)
+    lax.fori_loop(0, early, q_step, 0)
+
+    kv_copy().wait()
+    parts = kv_heads * 2
+    step_rows = kv_stage.shape[0]
+    rows_out = step_rows // parts
+
+    def separate(i, carry):
+        base = pl.multiple_of(i * step_rows, step_rows)
+        kv_stage[...] = kv_raw[pl.ds(base, step_rows), :].astype(f32)
+        to = pl.multiple_of(i * rows_out, rows_out)
+        for j in range(parts):
+            kv_w[pl.ds(to, rows_out), j * head_dim:(j + 1) * head_dim] = kv_stage[
+                pl.ds(j, rows_out, stride=parts), :
+            ].astype(bf16)
+        return carry
+
+    lax.fori_loop(0, depth // rows_out, separate, 0)
+    ship(q_chunks, project(lambda s: kv_w[s * feat:(s + 1) * feat, :]))
+    lax.fori_loop(early, q_chunks, q_step, 0)
 
     wo_rows = wout_hbm.shape[0]
     halves = depth // wo_rows
@@ -288,7 +297,7 @@
             f = fresh[n] * factor
             s = jnp.where(mask[n], scores[n] * factor, -1e30)
             top = jnp.maximum(jnp.max(s, axis=1, keepdims=True), f)
-            w = jnp.where(mask[n], jnp.exp(s - top), 0.0)
+            w = jnp.exp(s - top)
             fw = jnp.exp(f - top)
             whole = jnp.sum(w, axis=1, keepdims=True) + fw
             probs = (w / whole).astype(bf16)
@@ -427,6 +436,7 @@
             pltpu.VMEM((owners * kv_heads, slots, head_dim), bf16),
             pltpu.VMEM((ny, batch, feat), bf16),
             pltpu.VMEM((nx * ny, 8, lanes), f32),
+            pltpu.VMEM((depth // signs.shape[0], 2, batch, signs.shape[0]), f32),
             pltpu.VMEM((ny, batch, feat), bf16),
             pltpu.VMEM((q_chunks + 1, nx, owners, CHUNK), f32),
             pltpu.VMEM((q_chunks + 1, nx, owners, CHUNK), f32),

time: 49.3 us -> 49.3 us (level)
  no operation moved by 1% of the time
where the time goes in v4:
time: 49.3 us; the launch traced here: 49.2 us
  Pallas kernels  47.6 us (97%)
  local copies, waits for them, and re-layouts  1.57 us (3%)
    pallas_call x1, Pallas kernels, direct_body(): pl.pallas_call(functools.partial(decode_kernel, nx, ny, dims), out_shape=...  47.6 us
    unnamed x1, local copies, waits for them, and re-layouts  1.57 us

profile of v4, /device:TPU:0, one launch (start us, length us, event | category | flops | bytes accessed | tf_op | source)
XLA Modules:
  0.0 49.2 jit_solution(2467346852431699233)
XLA Ops:
  0.0 47.6 %shard_map.100 = bf16[64,1024]{1,0:T(8,128)(2,1)} custom-call(bf16[64,1024]{1,0:T(8,128)(2,1)} %hidden_ref.1, s32[32,64]{1,0:T(8,128)} %bitcast.9, s32[1,128]{1,0:T(1,128)} %bitcast.11, f32[1,128]{1,0:T(1,128)} %constant.2.clone.freq_ref, s32[1,16]{1,0:T(1,128)} %bitcast.10, s32[16]{0:T(128)} %len_ref.1, bf16[4096,2048]{1,0:T(8,128)(2,1)} %wq_hbm.1, ...), custom_call_target="tpu_custom_call" | custom-call | tf_op jit(solution)/shard_map/pallas_call | solution.py:425
  47.6 1.6 %copy.12 = bf16[64,1024]{1,0:T(8,128)(2,1)} copy(bf16[64,1024]{1,0:T(8,128)(2,1)} %shard_map.100) | data formatting | bytes 262144
